TPU v7x, 32 devices: a whole 2x2x4 slice. The times are simulated.
32 devices in a mesh: lat: 8 (over z, x), rad: 4 (over y, core).
Axes of the slice: x: 2, y: 2, z: 4, core: 2. Of those that a mesh axis runs over, the one named last changes fastest.
Arguments:
- kernel: bfloat16 [1024, 4, 64, 256], P(('lat', 'rad')), may hold values from -0.1875 to 0.1875
- target_device: int32 [1024, 4], P(('lat', 'rad')), may hold values from 0 to 31, all different within a row; in each aligned block of 32 rows (0 to 31, 32 to 63, ...) at most 8 rows name the same one
- target_block: int32 [1024, 4], P(('lat', 'rad')), may hold values from 0 to 127
- counts: int32 [1024], P(('lat', 'rad')), may hold values from 16 to 64
- traveltimes: float32 [1024, 64], P(('lat', 'rad')), may hold values from -6 to 6
- prior_residual: float32 [1024, 64], P(('lat', 'rad')), may hold values from -12 to 12
Outputs:
- model_update: float32 [32, 128, 256], P('rad', 'lat')
- data_vector: float32 [1024, 64], P(('lat', 'rad'))
Inputs may be any that keep to these rules, and one draw needn't show every extreme that they name: `target_device`: each ray block names 4 different devices; among the ray blocks of one device at most 8 name the same device, and some device is named by exactly 8 of them.
All inputs are finite; a program needn't handle non-finite values.
Results may differ from a plain program's by a relative error of at most 0.007.
Values may be sent and summed in bfloat16 or wider, within the bound.
A program may use at most 128 MiB of HBM per device.

v0:
```python
import jax
import jax.numpy as jnp
from jax import lax
from jax.sharding import PartitionSpec as P

ITERS = 3
MB_R = 8
MB_L = 16


FREEDOM = 4.0
DAMPING = 0.3


def extended(cells, sides, width):
    for axis, dim in sides:
        count = lax.axis_size(axis)
        ends = count - 1
        head = lax.slice_in_dim(cells, 0, width, axis=dim)
        tail = lax.slice_in_dim(cells, cells.shape[dim] - width, cells.shape[dim], axis=dim)
        cells = jnp.concatenate(
            [
                lax.ppermute(tail, axis, [(i, (i + 1) % count) for i in range(ends)]),
                cells,
                lax.ppermute(head, axis, [((i + 1) % count, i) for i in range(ends)]),
            ],
            axis=dim,
        )
    return cells


def roughen(model_field):
    padded = extended(model_field, (("lat", 1), ("rad", 0)), 1)
    beside = padded[2:, 1:-1] + padded[:-2, 1:-1] + padded[1:-1, 2:] + padded[1:-1, :-2]
    return 4.0 * model_field - beside


def data_norm(data_vector, pen_vec):
    totals = lax.psum(
        (jnp.sum(data_vector * data_vector), jnp.sum(pen_vec * pen_vec)), ("lat", "rad")
    )
    return jnp.sqrt(totals[0] + totals[1])


def model_norm(model_dir):
    return jnp.sqrt(lax.psum(jnp.sum(model_dir * model_dir), ("lat", "rad")))


def body(kernel, target_device, target_block, counts, traveltimes, prior_residual):
    devices = lax.axis_size("lat") * lax.axis_size("rad")
    ray_blocks, fanout, ray_len, cell_len = kernel.shape
    capacity = max(2, 2 * ray_blocks * fanout // devices)
    entries = ray_blocks * fanout
    num_blocks = MB_R * MB_L
    targets = target_device.reshape(entries)
    onehot = (targets[:, None] == jnp.arange(devices, dtype=jnp.int32)[None, :]).astype(jnp.int32)
    earlier = jnp.cumsum(onehot, axis=0) - onehot
    slot_rank = jnp.sum(earlier * onehot, axis=1)
    position = targets * capacity + slot_rank
    requests = (
        jnp.full((devices * capacity,), -1, jnp.int32)
        .at[position]
        .set(target_block.reshape(entries))
    )
    wanted = lax.all_to_all(
        requests.reshape(devices, capacity), ("lat", "rad"), split_axis=0, concat_axis=0, tiled=True
    )
    present = wanted >= 0
    segment = jnp.where(present, wanted, num_blocks).reshape(devices * capacity)
    safe_index = jnp.maximum(wanted, 0)

    def collect(arrived):
        summed = jax.ops.segment_sum(
            arrived.reshape(devices * capacity, cell_len), segment, num_segments=num_blocks + 1
        )
        return summed[:num_blocks].reshape(MB_R, MB_L, cell_len)

    outgoing = jnp.zeros((devices * capacity, ray_len, cell_len), jnp.bfloat16)
    outgoing = outgoing.at[position].set(kernel.reshape(entries, ray_len, cell_len))
    held_tiles = lax.all_to_all(
        outgoing.reshape(devices, capacity, ray_len, cell_len),
        ("lat", "rad"),
        split_axis=0,
        concat_axis=0,
        tiled=True,
    )

    def adjoint(ray_values):
        rounded = ray_values.astype(jnp.bfloat16)
        spread = jnp.zeros((devices * capacity, ray_len), jnp.bfloat16)
        spread = spread.at[position].set(jnp.repeat(rounded, fanout, axis=0))
        arrived = lax.all_to_all(
            spread.reshape(devices, capacity, ray_len),
            ("lat", "rad"),
            split_axis=0,
            concat_axis=0,
            tiled=True,
        )
        partial_value = jnp.einsum(
            "sqrc,sqr->sqc", held_tiles, arrived, preferred_element_type=jnp.float32
        )
        return collect(partial_value)

    ray_mask = (jnp.arange(ray_len, dtype=jnp.int32)[None, :] < counts[:, None]).astype(jnp.float32)
    weights = ray_mask * jnp.sqrt((FREEDOM + 1.0) / (FREEDOM + prior_residual * prior_residual))
    data_vector = weights * traveltimes
    pen_vec = jnp.zeros((MB_R, MB_L, cell_len), jnp.float32)
    beta_norm = data_norm(data_vector, pen_vec)
    data_vector = data_vector / beta_norm
    model_dir = adjoint(weights * data_vector)
    alpha_norm = model_norm(model_dir)
    model_dir = model_dir / alpha_norm
    search_dir = model_dir
    model_update = jnp.zeros_like(model_dir)
    phi_bar = beta_norm
    rho_bar = alpha_norm
    for sweep in range(ITERS):
        flat_model = model_dir.reshape(num_blocks, cell_len).astype(jnp.bfloat16)
        blocks = jnp.where(present[:, :, None], flat_model[safe_index], jnp.zeros((), jnp.bfloat16))
        products = jnp.einsum(
            "sqrc,sqc->sqr", held_tiles, blocks, preferred_element_type=jnp.float32
        )
        returned = lax.all_to_all(products, ("lat", "rad"), split_axis=0, concat_axis=0, tiled=True)
        picked = returned.reshape(devices * capacity, ray_len)[position]
        data_vector = (
            weights * jnp.sum(picked.reshape(ray_blocks, fanout, ray_len), axis=1)
            - alpha_norm * data_vector
        )
        pen_vec = DAMPING * roughen(model_dir) - alpha_norm * pen_vec
        beta_norm = data_norm(data_vector, pen_vec)
        data_vector = data_vector / beta_norm
        pen_vec = pen_vec / beta_norm
        model_dir = (
            adjoint(weights * data_vector) + DAMPING * roughen(pen_vec) - beta_norm * model_dir
        )
        alpha_norm = model_norm(model_dir)
        model_dir = model_dir / alpha_norm
        rho_value = jnp.sqrt(rho_bar * rho_bar + beta_norm * beta_norm)
        cosine = rho_bar / rho_value
        sine = beta_norm / rho_value
        theta_value = sine * alpha_norm
        rho_bar = -cosine * alpha_norm
        phi_value = cosine * phi_bar
        phi_bar = sine * phi_bar
        model_update = model_update + phi_value / rho_value * search_dir
        search_dir = model_dir - theta_value / rho_value * search_dir
    return (model_update, data_vector)


def solution(mesh):
    in_specs = (
        P(("lat", "rad"), None, None, None),
        P(("lat", "rad"), None),
        P(("lat", "rad"), None),
        P(("lat", "rad")),
        P(("lat", "rad"), None),
        P(("lat", "rad"), None),
    )
    out_specs = (P("rad", "lat", None), P(("lat", "rad"), None))
    return jax.shard_map(body, mesh=mesh, in_specs=in_specs, out_specs=out_specs, check_vma=False)
```

profile of v0, /device:TPU:0, one launch (start us, length us, event | category | flops | bytes accessed | tf_op | source)
XLA Modules:
  0.0 687.3 jit_solution(17505653479054844986)
XLA Ops:
  6.8 7.3 %all-to-all-start = ((s32[32,1,8]{2,1,0:T(1,128)}), s32[32,1,8]{2,1,0:T(1,128)S(1)}, u32[]{:S(2)}, u32[]{:S(2)}) async-start(s32[32,1,8]{2,1,0:T(1,128)} %bitcast.2), calls=%async_computation | async-start | bytes 32768 | tf_op jit(solution)/shard_map/all_to_all | solution.py:65
  14.1 40.8 %psum.88 = f32[]{:T(128)} all-reduce(f32[]{:T(128)} %multiply_reduce_fusion.8), channel_id=1, replica_groups=mesh['lat'=8,'rad'=4] {'lat','rad'}, use_global_device_ids=true, to_apply=%region_5.6 | all-reduce | flops 1 | bytes 8 | tf_op jit(solution)/shard_map/psum | solution.py:39
  58.1 4.7 all-to-all-start.2
  67.0 19.3 %scatter_fusion = bf16[256,64,256]{2,1,0:T(8,128)(2,1)} fusion(bf16[256,64,256]{2,1,0:T(8,128)(2,1)} %broadcast_in_dim.58, s32[128]{0:T(128)S(1)} %fusion.68, bf16[128,64,256]{2,1,0:T(8,128)(2,1)} %bitcast.83), kind=kCustom, calls=%fused_computation.7 | custom fusion | bytes 12583424 | tf_op jit(solution)/shard_map/scatter | solution.py:79
  86.3 6.0 all-to-all-start.1
  94.1 183.6 %all-to-all-done.1 = bf16[32,8,64,256]{3,2,1,0:T(8,128)(2,1)} async-done(((bf16[32,8,64,256]{3,2,1,0:T(8,128)(2,1)}), bf16[32,8,64,256]{3,2,1,0:T(8,128)(2,1)}, u32[]{:S(2)}, u32[]{:S(2)}) %all-to-all-start.1) | async-done | bytes 8388640 | tf_op jit(solution)/shard_map/all_to_all | solution.py:80
  277.6 4.6 fusion.56
  284.9 41.7 %psum.79 = f32[]{:T(128)} all-reduce(f32[]{:T(128)} %multiply_reduce_fusion.4), channel_id=1, replica_groups=mesh['lat'=8,'rad'=4] {'lat','rad'}, use_global_device_ids=true, to_apply=%region_10.11 | all-reduce | flops 1 | bytes 8 | tf_op jit(solution)/shard_map/psum | solution.py:46
  341.5 5.6 fusion.12
  347.9 5.3 all-to-all-start.3
  353.8 6.7 all-to-all-done.3
  364.6 38.3 %psum.89 = f32[]{:T(128)} all-reduce(f32[]{:T(128)S(6)} %add.151), channel_id=1, replica_groups=mesh['lat'=8,'rad'=4] {'lat','rad'}, use_global_device_ids=true, to_apply=%region_13.14 | all-reduce | flops 1 | bytes 8 | tf_op jit(solution)/shard_map/psum | solution.py:39
  411.0 5.1 all-to-all-start.4
  423.5 4.6 fusion.54
  430.8 38.5 %psum.82 = f32[]{:T(128)} all-reduce(f32[]{:T(128)} %get-tuple-element.14), channel_id=1, replica_groups=mesh['lat'=8,'rad'=4] {'lat','rad'}, use_global_device_ids=true, to_apply=%region_19.20 | all-reduce | flops 1 | bytes 8 | tf_op jit(solution)/shard_map/psum | solution.py:46
  484.1 5.6 fusion.9
  495.5 6.7 all-to-all-done.5
  505.7 38.3 %psum.90 = f32[]{:T(128)} all-reduce(f32[]{:T(128)S(6)} %add.160), channel_id=1, replica_groups=mesh['lat'=8,'rad'=4] {'lat','rad'}, use_global_device_ids=true, to_apply=%region_22.23 | all-reduce | flops 1 | bytes 8 | tf_op jit(solution)/shard_map/psum | solution.py:39
  552.2 5.1 all-to-all-start.6
  564.6 4.6 fusion.52
  571.9 38.5 %psum.85 = f32[]{:T(128)} all-reduce(f32[]{:T(128)} %get-tuple-element.6), channel_id=1, replica_groups=mesh['lat'=8,'rad'=4] {'lat','rad'}, use_global_device_ids=true, to_apply=%region_28.29 | all-reduce | flops 1 | bytes 8 | tf_op jit(solution)/shard_map/psum | solution.py:46
  625.2 5.6 fusion.6
  636.5 6.6 all-to-all-done.7
  646.8 38.3 %psum.91 = f32[]{:T(128)} all-reduce(f32[]{:T(128)S(6)} %add.170), channel_id=1, replica_groups=mesh['lat'=8,'rad'=4] {'lat','rad'}, use_global_device_ids=true, to_apply=%region_31.32 | all-reduce | flops 1 | bytes 8 | tf_op jit(solution)/shard_map/psum | solution.py:39
  (147 shorter events, 115.3 us)
Async XLA Ops:
  6.8 51.2 %all-to-all-start = ((s32[32,1,8]{2,1,0:T(1,128)}), s32[32,1,8]{2,1,0:T(1,128)S(1)}, u32[]{:S(2)}, u32[]{:S(2)}) async-start(s32[32,1,8]{2,1,0:T(1,128)} %bitcast.2), calls=%async_computation | async-start | bytes 32768 | tf_op jit(solution)/shard_map/all_to_all | solution.py:65
  58.1 28.3 %all-to-all-start.2 = ((bf16[32,2,256]{2,1,0:T(2,128)(2,1)}), bf16[32,2,256]{2,1,0:T(2,128)(2,1)S(1)}, u32[]{:S(2)}, u32[]{:S(2)}) async-start(bf16[32,2,256]{2,1,0:T(2,128)(2,1)} %reshape.318), calls=%async_computation.2 | async-start | bytes 65536 | tf_op jit(solution)/shard_map/all_to_all | solution.py:92
  86.3 191.3 %all-to-all-start.1 = ((bf16[32,8,64,256]{3,2,1,0:T(8,128)(2,1)}), bf16[32,8,64,256]{3,2,1,0:T(8,128)(2,1)}, u32[]{:S(2)}, u32[]{:S(2)}) async-start(bf16[32,8,64,256]{3,2,1,0:T(8,128)(2,1)} %bitcast.80), calls=%async_computation.1 | async-start | bytes 16777216 | tf_op jit(solution)/shard_map/all_to_all | solution.py:80
  327.3 6.8 collective-permute-start
  337.1 16.0 %collective-permute-start.2 = (f32[1,18,256]{2,1,0:T(8,128)S(1)}, f32[1,18,256]{2,1,0:T(8,128)S(1)}, u32[]{:S(2)}, u32[]{:S(2)}) collective-permute-start(f32[1,18,256]{2,1,0:T(8,128)S(1)} %get-tuple-element.30), channel_id=1, source_target_pairs={{1,0},{2,1},{3,2},{5,4},{6,5},{7,6},{9,8},{10,9},{11,10},{13,12},{... | collective-permute-start | bytes 55304 | tf_op jit(solution)/shard_map/ppermute | solution.py:25
  338.4 14.7 %collective-permute-start.3 = (f32[1,18,256]{2,1,0:T(8,128)S(1)}, f32[1,18,256]{2,1,0:T(8,128)S(1)}, u32[]{:S(2)}, u32[]{:S(2)}) collective-permute-start(f32[1,18,256]{2,1,0:T(8,128)S(1)} %get-tuple-element.31), channel_id=1, source_target_pairs={{0,1},{1,2},{2,3},{4,5},{5,6},{6,7},{8,9},{9,10},{10,11},{12,13},{... | collective-permute-start | bytes 55304 | tf_op jit(solution)/shard_map/ppermute | solution.py:23
  347.9 12.7 %all-to-all-start.3 = ((f32[32,1,512]{2,1,0:T(1,128)}), f32[32,1,512]{2,1,0:T(1,128)S(1)}, u32[]{:S(2)}, u32[]{:S(2)}) async-start(f32[32,1,512]{2,1,0:T(1,128)} %reshape.320), calls=%async_computation.3 | async-start | bytes 131072 | tf_op jit(solution)/shard_map/all_to_all | solution.py:123
  403.7 12.5 %collective-permute-start.4 = (f32[8,1,256]{2,1,0:T(1,128)S(1)}, f32[8,1,256]{2,1,0:T(1,128)S(1)}, u32[]{:S(2)}, u32[]{:S(2)}) collective-permute-start(f32[8,1,256]{2,1,0:T(1,128)S(1)} %get-tuple-element.39), channel_id=1, source_target_pairs={{0,4},{4,8},{8,12},{12,16},{16,20},{20,24},{24,28},{1,5},{5,9},{9,... | collective-permute-start | bytes 24584 | tf_op jit(solution)/shard_map/ppermute | solution.py:23
  407.9 8.3 %collective-permute-start.5 = (f32[8,1,256]{2,1,0:T(1,128)S(1)}, f32[8,1,256]{2,1,0:T(1,128)S(1)}, u32[]{:S(2)}, u32[]{:S(2)}) collective-permute-start(f32[8,1,256]{2,1,0:T(1,128)S(1)} %get-tuple-element.38), channel_id=1, source_target_pairs={{4,0},{8,4},{12,8},{16,12},{20,16},{24,20},{28,24},{5,1},{9,5},{13... | collective-permute-start | bytes 24584 | tf_op jit(solution)/shard_map/ppermute | solution.py:25
  411.0 12.3 %all-to-all-start.4 = ((bf16[32,2,256]{2,1,0:T(2,128)(2,1)}), bf16[32,2,256]{2,1,0:T(2,128)(2,1)S(1)}, u32[]{:S(2)}, u32[]{:S(2)}) async-start(bf16[32,2,256]{2,1,0:T(2,128)(2,1)} %reshape.322), calls=%async_computation.4 | async-start | bytes 65536 | tf_op jit(solution)/shard_map/all_to_all | solution.py:92
  416.2 13.9 %collective-permute-start.6 = (f32[1,18,256]{2,1,0:T(8,128)S(1)}, f32[1,18,256]{2,1,0:T(8,128)S(1)}, u32[]{:S(2)}, u32[]{:S(2)}) collective-permute-start(f32[1,18,256]{2,1,0:T(8,128)S(1)} %get-tuple-element.28), channel_id=1, source_target_pairs={{1,0},{2,1},{3,2},{5,4},{6,5},{7,6},{9,8},{10,9},{11,10},{13,12},{... | collective-permute-start | bytes 55304 | tf_op jit(solution)/shard_map/ppermute | solution.py:25
  417.7 12.4 %collective-permute-start.7 = (f32[1,18,256]{2,1,0:T(8,128)S(1)}, f32[1,18,256]{2,1,0:T(8,128)S(1)}, u32[]{:S(2)}, u32[]{:S(2)}) collective-permute-start(f32[1,18,256]{2,1,0:T(8,128)S(1)} %get-tuple-element.29), channel_id=1, source_target_pairs={{0,1},{1,2},{2,3},{4,5},{5,6},{6,7},{8,9},{9,10},{10,11},{12,13},{... | collective-permute-start | bytes 55304 | tf_op jit(solution)/shard_map/ppermute | solution.py:23
  479.8 15.0 %collective-permute-start.10 = (f32[1,18,256]{2,1,0:T(8,128)S(1)}, f32[1,18,256]{2,1,0:T(8,128)S(1)}, u32[]{:S(2)}, u32[]{:S(2)}) collective-permute-start(f32[1,18,256]{2,1,0:T(8,128)S(1)} %get-tuple-element.26), channel_id=1, source_target_pairs={{1,0},{2,1},{3,2},{5,4},{6,5},{7,6},{9,8},{10,9},{11,10},{13,12},{... | collective-permute-start | bytes 55304 | tf_op jit(solution)/shard_map/ppermute | solution.py:25
  481.1 13.8 %collective-permute-start.11 = (f32[1,18,256]{2,1,0:T(8,128)S(1)}, f32[1,18,256]{2,1,0:T(8,128)S(1)}, u32[]{:S(2)}, u32[]{:S(2)}) collective-permute-start(f32[1,18,256]{2,1,0:T(8,128)S(1)} %get-tuple-element.27), channel_id=1, source_target_pairs={{0,1},{1,2},{2,3},{4,5},{5,6},{6,7},{8,9},{9,10},{10,11},{12,13},{... | collective-permute-start | bytes 55304 | tf_op jit(solution)/shard_map/ppermute | solution.py:23
  490.5 11.7 %all-to-all-start.5 = ((f32[32,1,512]{2,1,0:T(1,128)}), f32[32,1,512]{2,1,0:T(1,128)S(1)}, u32[]{:S(2)}, u32[]{:S(2)}) async-start(f32[32,1,512]{2,1,0:T(1,128)} %reshape.324), calls=%async_computation.5 | async-start | bytes 131072 | tf_op jit(solution)/shard_map/all_to_all | solution.py:123
  544.8 12.5 %collective-permute-start.12 = (f32[8,1,256]{2,1,0:T(1,128)S(1)}, f32[8,1,256]{2,1,0:T(1,128)S(1)}, u32[]{:S(2)}, u32[]{:S(2)}) collective-permute-start(f32[8,1,256]{2,1,0:T(1,128)S(1)} %get-tuple-element.35), channel_id=1, source_target_pairs={{0,4},{4,8},{8,12},{12,16},{16,20},{20,24},{24,28},{1,5},{5,9},{9,... | collective-permute-start | bytes 24584 | tf_op jit(solution)/shard_map/ppermute | solution.py:23
  549.0 8.3 %collective-permute-start.13 = (f32[8,1,256]{2,1,0:T(1,128)S(1)}, f32[8,1,256]{2,1,0:T(1,128)S(1)}, u32[]{:S(2)}, u32[]{:S(2)}) collective-permute-start(f32[8,1,256]{2,1,0:T(1,128)S(1)} %get-tuple-element.34), channel_id=1, source_target_pairs={{4,0},{8,4},{12,8},{16,12},{20,16},{24,20},{28,24},{5,1},{9,5},{13... | collective-permute-start | bytes 24584 | tf_op jit(solution)/shard_map/ppermute | solution.py:25
  552.2 12.3 %all-to-all-start.6 = ((bf16[32,2,256]{2,1,0:T(2,128)(2,1)}), bf16[32,2,256]{2,1,0:T(2,128)(2,1)S(1)}, u32[]{:S(2)}, u32[]{:S(2)}) async-start(bf16[32,2,256]{2,1,0:T(2,128)(2,1)} %reshape.326), calls=%async_computation.6 | async-start | bytes 65536 | tf_op jit(solution)/shard_map/all_to_all | solution.py:92
  557.3 13.9 %collective-permute-start.14 = (f32[1,18,256]{2,1,0:T(8,128)S(1)}, f32[1,18,256]{2,1,0:T(8,128)S(1)}, u32[]{:S(2)}, u32[]{:S(2)}) collective-permute-start(f32[1,18,256]{2,1,0:T(8,128)S(1)} %get-tuple-element.24), channel_id=1, source_target_pairs={{1,0},{2,1},{3,2},{5,4},{6,5},{7,6},{9,8},{10,9},{11,10},{13,12},{... | collective-permute-start | bytes 55304 | tf_op jit(solution)/shard_map/ppermute | solution.py:25
  558.6 12.6 %collective-permute-start.15 = (f32[1,18,256]{2,1,0:T(8,128)S(1)}, f32[1,18,256]{2,1,0:T(8,128)S(1)}, u32[]{:S(2)}, u32[]{:S(2)}) collective-permute-start(f32[1,18,256]{2,1,0:T(8,128)S(1)} %get-tuple-element.25), channel_id=1, source_target_pairs={{0,1},{1,2},{2,3},{4,5},{5,6},{6,7},{8,9},{9,10},{10,11},{12,13},{... | collective-permute-start | bytes 55304 | tf_op jit(solution)/shard_map/ppermute | solution.py:23
  611.1 7.0 %collective-permute-start.16 = (f32[8,1,256]{2,1,0:T(1,128)S(1)}, f32[8,1,256]{2,1,0:T(1,128)S(1)}, u32[]{:S(2)}, u32[]{:S(2)}) collective-permute-start(f32[8,1,256]{2,1,0:T(1,128)S(1)} %get-tuple-element.33), channel_id=1, source_target_pairs={{0,4},{4,8},{8,12},{12,16},{16,20},{20,24},{24,28},{1,5},{5,9},{9,... | collective-permute-start | bytes 24584 | tf_op jit(solution)/shard_map/ppermute | solution.py:23
  620.9 14.9 %collective-permute-start.18 = (f32[1,18,256]{2,1,0:T(8,128)S(1)}, f32[1,18,256]{2,1,0:T(8,128)S(1)}, u32[]{:S(2)}, u32[]{:S(2)}) collective-permute-start(f32[1,18,256]{2,1,0:T(8,128)S(1)} %get-tuple-element.22), channel_id=1, source_target_pairs={{1,0},{2,1},{3,2},{5,4},{6,5},{7,6},{9,8},{10,9},{11,10},{13,12},{... | collective-permute-start | bytes 55304 | tf_op jit(solution)/shard_map/ppermute | solution.py:25
  622.2 13.6 %collective-permute-start.19 = (f32[1,18,256]{2,1,0:T(8,128)S(1)}, f32[1,18,256]{2,1,0:T(8,128)S(1)}, u32[]{:S(2)}, u32[]{:S(2)}) collective-permute-start(f32[1,18,256]{2,1,0:T(8,128)S(1)} %get-tuple-element.23), channel_id=1, source_target_pairs={{0,1},{1,2},{2,3},{4,5},{5,6},{6,7},{8,9},{9,10},{10,11},{12,13},{... | collective-permute-start | bytes 55304 | tf_op jit(solution)/shard_map/ppermute | solution.py:23
  631.6 11.5 %all-to-all-start.7 = ((f32[32,1,512]{2,1,0:T(1,128)}), f32[32,1,512]{2,1,0:T(1,128)S(1)}, u32[]{:S(2)}, u32[]{:S(2)}) async-start(f32[32,1,512]{2,1,0:T(1,128)} %reshape.328), calls=%async_computation.7 | async-start | bytes 131072 | tf_op jit(solution)/shard_map/all_to_all | solution.py:123
  (7 other events, 264.9 us)
where the time goes:
time: 690 us; the launch traced here: 687 us
  blocking collectives  274 us (40%)
  waiting for transfers between devices  218 us (32%)
  starting transfers between devices  91.2 us (13%)
  local copies, waits for them, and re-layouts  42 us (6%)
  matrix products  30.6 us (4%)
  other arithmetic  20.6 us (3%)
  between operations  10.6 us (2%)
    all_to_all x1, waiting for transfers between devices, body(): lax.all_to_all(outgoing.reshape(devices, capacity, ray_len, cell_len), ('...  184 us
    psum x4, blocking collectives, data_norm(): lax.psum((jnp.sum(data_vector * data_vector), jnp.sum(pen_vec * pen_vec))...  156 us
    psum x3, blocking collectives, model_norm(): return jnp.sqrt(lax.psum(jnp.sum(model_dir * model_dir), ('lat', 'rad')))  119 us
    ppermute x10, starting transfers between devices, extended(): lax.ppermute(tail, axis, [(i, (i + 1) % count) for i in range(ends)])  36.1 us
    all_to_all x3, waiting for transfers between devices, body(): lax.all_to_all(products, ('lat', 'rad'), split_axis=0, concat_axis=0, til...  20.1 us
    scatter x1, local copies, waits for them, and re-layouts, body(): outgoing.at[position].set(kernel.reshape(entries, ray_len, cell_len))  19.3 us
    dot_general x3, matrix products, body(): jnp.einsum('sqrc,sqc->sqr', held_tiles, blocks, preferred_element_type=jn...  16.9 us
    all_to_all x3, starting transfers between devices, adjoint(): lax.all_to_all(spread.reshape(devices, capacity, ray_len), ('lat', 'rad')...  14.8 us
  transfers between devices with their start and end apart: 28, of which 9 were waited for; matrix products, arithmetic and copies ran while one was open for 10% of the time, Pallas kernels for 0%

commit v1 on v0

v1 whole, which is shorter than its diff:
```python
import functools

import jax
import jax.numpy as jnp
from jax import lax
from jax.experimental import pallas as pl
from jax.experimental.pallas import tpu as pltpu
from jax.sharding import PartitionSpec as P

ITERS = 3
MB_R = 8
MB_L = 16
FREEDOM = 4.0
DAMPING = 0.3
LANES = 128
GROUP = 8

F32 = jnp.float32
BF16 = jnp.bfloat16
MESH = pl.DeviceIdType.MESH


def iota(shape, dim):
    return lax.broadcasted_iota(jnp.int32, shape, dim)


def onehot(cond):
    return jnp.where(cond, 1.0, 0.0).astype(BF16)


def lsqr_kernel(
    n_lat, n_rad, slots,
    kernel_ref, target_ref, block_ref, counts_ref, times_ref, prior_ref,
    update_ref, data_ref,
    tiles, send, recv, sum_send, sum_recv, edge_send, edge_recv, ids_send, ids_recv,
    tile_sem, send_sem, recv_sem, sum_send_sem, sum_recv_sem, edge_send_sem, edge_recv_sem,
    ids_send_sem, ids_recv_sem,
):
    n = n_lat * n_rad
    rays_b, fanout, ray_len, cells = tiles.shape
    entries = rays_b * fanout
    halves = cells // LANES
    rows = halves * slots
    num_blocks = MB_R * MB_L
    groups = rays_b // GROUP
    width = GROUP * ray_len
    lat, rad = lax.axis_index("lat"), lax.axis_index("rad")
    me = lat * n_rad + rad

    def at(peer):
        return (peer // n_rad, peer % n_rad)

    def shifted(step):
        return at(lax.rem(me + step, n))

    barrier = pltpu.get_barrier_semaphore()

    def greet(step, carry):
        pl.semaphore_signal(barrier, inc=1, device_id=shifted(step), device_id_type=MESH)
        return carry

    lax.fori_loop(1, n, greet, 0)

    def tile_copy(g):
        part = pl.ds(g * GROUP, GROUP)
        return pltpu.make_async_copy(kernel_ref.at[part], tiles.at[part], tile_sem.at[g])

    for g in range(groups):
        tile_copy(g).start()

    named = jnp.concatenate([target_ref[:, k:k + 1] for k in range(fanout)], axis=0)
    wanted = jnp.concatenate([block_ref[:, k:k + 1] for k in range(fanout)], axis=0)
    away = named - me
    away = jnp.where(away < 0, away + n, away)
    square = (entries, entries)
    away_col = jnp.broadcast_to(away.astype(F32), square)
    away_row = away_col.T
    earlier = (away_col == away_row) & (iota(square, 1) < iota(square, 0))
    rank = jnp.sum(jnp.where(earlier, 1.0, 0.0), axis=1, keepdims=True)
    place_col = away.astype(F32) * rows + rank
    place_row = jnp.broadcast_to(place_col, square).T[0:1, :]
    place_cols = jnp.concatenate([place_col + h * slots for h in range(halves)], axis=0)
    place_rows = jnp.concatenate([place_row + h * slots for h in range(halves)], axis=1)
    pick = onehot(
        iota((halves * entries, n * rows), 1) == place_cols.astype(jnp.int32)
    )
    spread = onehot(
        iota((n * rows, halves * entries), 0) == place_rows.astype(jnp.int32)
    )
    partner = onehot(iota((n, entries), 0) == away_row[0:1, :].astype(jnp.int32))
    marks = jnp.where(
        iota((entries, LANES), 1) == rank.astype(jnp.int32), (wanted + 1).astype(F32), 0.0
    ).astype(BF16)
    ids = jnp.dot(partner, marks, preferred_element_type=F32)

    lane = iota((GROUP, width), 1)
    own = (lane // ray_len) == iota((GROUP, width), 0)
    ray = lane % ray_len
    eye = iota((rays_b, rays_b), 0) == iota((rays_b, rays_b), 1)
    count = jnp.sum(
        jnp.where(eye, jnp.broadcast_to(counts_ref[...], (rays_b, rays_b)).astype(F32), 0.0),
        axis=1, keepdims=True,
    ).astype(jnp.int32)

    def repeated(ref, g):
        part = ref[g * GROUP:(g + 1) * GROUP, :]
        return jnp.concatenate([part] * GROUP, axis=1)

    weights, data = [], []
    for g in range(groups):
        prior = repeated(prior_ref, g)
        valid = own & (ray < count[g * GROUP:(g + 1) * GROUP])
        w = jnp.where(valid, jnp.sqrt((FREEDOM + 1.0) / (FREEDOM + prior * prior)), 0.0)
        weights.append(w)
        data.append(w * repeated(times_ref, g))

    def total(parts):
        acc = parts[0] * parts[0]
        for p in parts[1:]:
            acc = acc + p * p
        return jnp.sum(jnp.sum(acc, axis=0, keepdims=True), axis=1, keepdims=True)

    pl.semaphore_wait(barrier, n - 1)

    def exchange(src, dst, size, s_sem, r_sem):
        def go(step, carry):
            back = n - step
            pltpu.make_async_remote_copy(
                src_ref=src.at[pl.ds(pl.multiple_of(step * size, size), size)],
                dst_ref=dst.at[pl.ds(pl.multiple_of(back * size, size), size)],
                send_sem=s_sem, recv_sem=r_sem,
                device_id=shifted(step), device_id_type=MESH,
            ).start()
            return carry
        lax.fori_loop(1, n, go, 0)

    def arrived(dst, size, sem):
        part = dst.at[pl.ds(size, (n - 1) * size)]
        pltpu.make_async_copy(part, part, sem).wait()

    def send_sum(i, value):
        row = jnp.broadcast_to(value, (1, LANES))
        sum_send[i] = row
        sum_recv[i, 0] = row
        src, dst = sum_send.at[i], sum_recv.at[i]

        def go(step, carry):
            pltpu.make_async_remote_copy(
                src_ref=src, dst_ref=dst.at[n - step],
                send_sem=sum_send_sem.at[i], recv_sem=sum_recv_sem.at[i],
                device_id=shifted(step), device_id_type=MESH,
            ).start()
            return carry
        lax.fori_loop(1, n, go, 0)

    def get_sum(i):
        arrived(sum_recv.at[i], 1, sum_recv_sem.at[i])
        return jnp.sum(sum_recv[i], axis=0)[:, 0:1]

    field4 = (halves, MB_R, MB_L, LANES)
    field = (halves * num_blocks, LANES)
    radial, lateral = halves * MB_L, halves * MB_R
    edge_parts = ((0, radial), (radial, radial), (2 * radial, lateral), (2 * radial + lateral, lateral))
    up = (lat, lax.rem(rad + n_rad - 1, n_rad))
    down = (lat, lax.rem(rad + 1, n_rad))
    left = (lax.rem(lat + n_lat - 1, n_lat), rad)
    right = (lax.rem(lat + 1, n_lat), rad)

    def send_edges(i, x):
        x4 = x.reshape(field4)
        edge_send[i, 0:radial] = x4[:, 0].reshape(radial, LANES)
        edge_send[i, radial:2 * radial] = x4[:, MB_R - 1].reshape(radial, LANES)
        edge_send[i, 2 * radial:2 * radial + lateral] = x4[:, :, 0].reshape(lateral, LANES)
        edge_send[i, 2 * radial + lateral:] = x4[:, :, MB_L - 1].reshape(lateral, LANES)
        for a, b, device in ((0, 1, up), (1, 0, down), (2, 3, left), (3, 2, right)):
            pltpu.make_async_remote_copy(
                src_ref=edge_send.at[i, pl.ds(*edge_parts[a])],
                dst_ref=edge_recv.at[i, pl.ds(*edge_parts[b])],
                send_sem=edge_send_sem.at[i], recv_sem=edge_recv_sem.at[i],
                device_id=device, device_id_type=MESH,
            ).start()

    def roughen(i, x):
        whole = edge_recv.at[i]
        pltpu.make_async_copy(whole, whole, edge_recv_sem.at[i]).wait()

        def edge(part, outside):
            start, size = edge_parts[part]
            return jnp.where(outside, 0.0, edge_recv[i, start:start + size])

        above = edge(0, rad == 0).reshape(halves, 1, MB_L, LANES)
        below = edge(1, rad == n_rad - 1).reshape(halves, 1, MB_L, LANES)
        before = edge(2, lat == 0)
        after = edge(3, lat == n_lat - 1)
        x4 = x.reshape(field4)
        radials = jnp.concatenate([above, x4[:, :-1]], axis=1) + jnp.concatenate(
            [x4[:, 1:], below], axis=1
        )

        def along(e):
            return jnp.broadcast_to(e[:, None, :], (lateral, MB_L, LANES)).reshape(field)

        block_l = iota(field, 0) % MB_L
        prev = jnp.where(block_l == 0, along(before), pltpu.roll(x, 1, 0))
        nxt = jnp.where(block_l == MB_L - 1, along(after), pltpu.roll(x, field[0] - 1, 0))
        return 4.0 * x - (radials.reshape(field) + prev + nxt)

    def tile_part(g, k):
        return tiles[g * GROUP:(g + 1) * GROUP, k].reshape(width, cells)

    def send_rows(i, values):
        send[i] = values.astype(BF16)
        recv[i, 0:rows] = send[i, 0:rows]
        exchange(send.at[i], recv.at[i], rows, send_sem.at[i], recv_sem.at[i])

    def adjoint(i, ray_values, first=False):
        parts = [[None] * groups for _ in range(fanout)]
        for g in range(groups):
            if first:
                tile_copy(g).wait()
            y = ray_values[g].astype(BF16)
            for k in range(fanout):
                parts[k][g] = jnp.dot(y, tile_part(g, k), preferred_element_type=F32)
        flat = [p for k in range(fanout) for p in parts[k]]
        stacked = jnp.concatenate(
            [p[:, h * LANES:(h + 1) * LANES] for h in range(halves) for p in flat], axis=0
        ).astype(BF16)
        send_rows(i, jnp.dot(spread, stacked, preferred_element_type=F32))

    def forward(i):
        arrived(recv.at[i], rows, recv_sem.at[i])
        blocks = jnp.dot(pick, recv[i], preferred_element_type=F32)
        out = []
        for g in range(groups):
            acc = None
            for k in range(fanout):
                at_row = k * rays_b + g * GROUP
                v = jnp.concatenate(
                    [
                        blocks[h * entries + at_row:h * entries + at_row + GROUP]
                        for h in range(halves)
                    ],
                    axis=1,
                ).astype(BF16)
                term = lax.dot_general(
                    v, tile_part(g, k), (((1,), (1,)), ((), ())), preferred_element_type=F32
                )
                acc = term if acc is None else acc + term
            out.append(acc)
        return out

    first_sum = total(data)
    id_rows = jnp.where(iota((n, LANES), 1) == slots, first_sum, ids)
    ids_send[...] = id_rows.reshape(n, 1, LANES)
    ids_recv[0] = ids_send[0]
    exchange(ids_send, ids_recv, 1, ids_send_sem, ids_recv_sem)

    adjoint(0, [w * d for w, d in zip(weights, data)], first=True)

    arrived(ids_recv, 1, ids_recv_sem)
    got = ids_recv[...].reshape(n, LANES)
    beta = jnp.sqrt(jnp.sum(got, axis=0, keepdims=True)[:, slots:slots + 1])
    slot_rows = (n * rows, LANES)
    each = jnp.broadcast_to(got[:, None, :], (n, rows, LANES)).reshape(slot_rows)
    each = jnp.where(iota(slot_rows, 1) == iota(slot_rows, 0) % slots, each, 0.0)
    block_id = jnp.sum(each, axis=1, keepdims=True).astype(jnp.int32)
    asked = jnp.where(iota(slot_rows, 1) + 1 == block_id, 1.0, 0.0)
    half = (iota(slot_rows, 0) % rows) // slots
    served = jnp.concatenate([jnp.where(half == h, asked, 0.0) for h in range(halves)], axis=1)
    gather = served.astype(BF16)
    collect = served.T.astype(BF16)

    def collected(i):
        arrived(recv.at[i], rows, recv_sem.at[i])
        return jnp.dot(collect, recv[i], preferred_element_type=F32)

    x = collected(0) / beta
    data = [d / beta for d in data]
    phi_bar = beta
    round_i, sum_i, edge_i = 1, 0, 0
    pen = search = update = None
    for sweep in range(ITERS):
        send_rows(round_i, jnp.dot(gather, x.astype(BF16), preferred_element_type=F32))
        send_edges(edge_i, x)
        send_sum(sum_i, total([x]))
        products = forward(round_i)
        alpha = jnp.sqrt(get_sum(sum_i))
        inverse = 1.0 / alpha
        data = [w * (p * inverse) - alpha * d for w, p, d in zip(weights, products, data)]
        v = x * inverse
        pen_new = (DAMPING * inverse) * roughen(edge_i, x)
        pen = pen_new if pen is None else pen_new - alpha * pen
        round_i, sum_i, edge_i = round_i + 1, sum_i + 1, edge_i + 1
        if sweep == 0:
            search = v
            rho_bar = alpha
        else:
            search = v - (sine * alpha / rho) * search
            rho_bar = -cosine * alpha
        last = sweep == ITERS - 1
        acc = total(data) + total([pen])
        send_sum(sum_i, acc)
        if not last:
            send_edges(edge_i, pen)
            adjoint(round_i, [w * d for w, d in zip(weights, data)])
        beta = jnp.sqrt(get_sum(sum_i))
        inverse = 1.0 / beta
        data = [d * inverse for d in data]
        rho = jnp.sqrt(rho_bar * rho_bar + beta * beta)
        cosine, sine = rho_bar / rho, beta / rho
        phi = cosine * phi_bar
        phi_bar = sine * phi_bar
        step = (phi / rho) * search
        update = step if update is None else update + step
        if not last:
            rough = DAMPING * roughen(edge_i, pen)
            pen = pen * inverse
            x = (collected(round_i) + rough) * inverse - beta * v
            round_i, edge_i = round_i + 1, edge_i + 1
        sum_i += 1

    for h in range(halves):
        part = update[h * num_blocks:(h + 1) * num_blocks]
        update_ref[:, :, h * LANES:(h + 1) * LANES] = part.reshape(MB_R, MB_L, LANES)
    for g in range(groups):
        acc = data[g][:, 0:ray_len]
        for i in range(1, GROUP):
            acc = acc + data[g][:, i * ray_len:(i + 1) * ray_len]
        data_ref[g * GROUP:(g + 1) * GROUP, :] = acc

    def left_buffer(ref, sem):
        pltpu.make_async_copy(ref, ref, sem).wait()

    left_buffer(ids_send.at[pl.ds(1, n - 1)], ids_send_sem)
    for i in range(2 * ITERS):
        left_buffer(send.at[i, pl.ds(rows, (n - 1) * rows)], send_sem.at[i])
    for i in range(2 * ITERS):
        left_buffer(sum_recv.at[i, pl.ds(1, n - 1)], sum_send_sem.at[i])
    for i in range(2 * ITERS - 1):
        left_buffer(edge_send.at[i], edge_send_sem.at[i])


def body(kernel, target_device, target_block, counts, traveltimes, prior_residual):
    n_lat, n_rad = lax.axis_size("lat"), lax.axis_size("rad")
    n = n_lat * n_rad
    rays_b, fanout, ray_len, cells = kernel.shape
    capacity = max(2, 2 * rays_b * fanout // n)
    slots = -(-capacity // 8) * 8
    halves = cells // LANES
    rows = halves * slots
    edges = 2 * halves * (MB_R + MB_L)
    payloads, sums, fields = 2 * ITERS, 2 * ITERS, 2 * ITERS - 1
    dma = pltpu.SemaphoreType.DMA
    vmem = pl.BlockSpec(memory_space=pltpu.VMEM)
    return pl.pallas_call(
        functools.partial(lsqr_kernel, n_lat, n_rad, slots),
        out_shape=(
            jax.ShapeDtypeStruct((MB_R, MB_L, cells), F32),
            jax.ShapeDtypeStruct((rays_b, ray_len), F32),
        ),
        in_specs=[pl.BlockSpec(memory_space=pl.ANY)] + [vmem] * 5,
        out_specs=(vmem, vmem),
        scratch_shapes=[
            pltpu.VMEM(kernel.shape, BF16),
            pltpu.VMEM((payloads, n * rows, LANES), BF16),
            pltpu.VMEM((payloads, n * rows, LANES), BF16),
            pltpu.VMEM((sums, 1, LANES), F32),
            pltpu.VMEM((sums, n, 1, LANES), F32),
            pltpu.VMEM((fields, edges, LANES), F32),
            pltpu.VMEM((fields, edges, LANES), F32),
            pltpu.VMEM((n, 1, LANES), F32),
            pltpu.VMEM((n, 1, LANES), F32),
            dma((rays_b // GROUP,)),
            dma((payloads,)), dma((payloads,)),
            dma((sums,)), dma((sums,)),
            dma((fields,)), dma((fields,)),
            dma, dma,
        ],
        compiler_params=pltpu.CompilerParams(
            collective_id=0, has_side_effects=True, vmem_limit_bytes=48 * 1024 * 1024
        ),
        cost_estimate=pl.CostEstimate(
            flops=14 * kernel.size, bytes_accessed=2 * kernel.size, transcendentals=0
        ),
    )(kernel, target_device, target_block, counts.reshape(1, rays_b), traveltimes, prior_residual)


def solution(mesh):
    in_specs = (
        P(("lat", "rad"), None, None, None),
        P(("lat", "rad"), None),
        P(("lat", "rad"), None),
        P(("lat", "rad")),
        P(("lat", "rad"), None),
        P(("lat", "rad"), None),
    )
    out_specs = (P("rad", "lat", None), P(("lat", "rad"), None))
    return jax.shard_map(body, mesh=mesh, in_specs=in_specs, out_specs=out_specs, check_vma=False)
```

time: 690 us -> 65.5 us (0.09)
  blocking collectives: 274 us -> 0 us
  waiting for transfers between devices: 218 us -> 0 us
  starting transfers between devices: 91.2 us -> 0 us
  Pallas kernels: 0 us -> 57.4 us
  local copies, waits for them, and re-layouts: 42 us -> 7.06 us
  matrix products: 30.6 us -> 0 us
  other arithmetic: 20.6 us -> 0 us
  between operations: 10.6 us -> 0.64 us
    psum x7 -> x0, blocking collectives: 274 us -> none  [the longest x4 156 us: data_norm(): lax.psum((jnp.sum(data_vector * data_vector), jnp.sum(pen_vec * pen_vec))...]
    all_to_all x8 -> x0, waiting for transfers between devices: 209 us -> none  [the longest x1 184 us: body(): lax.all_to_all(outgoing.reshape(devices, capacity, ray_len, cell_len), ('...]
    pallas_call x0 -> x1, Pallas kernels: none -> 57.4 us  [body(): pl.pallas_call(functools.partial(lsqr_kernel, n_lat, n_rad, slots), out_s...]
    ppermute x20 -> x0, starting transfers between devices: 49.4 us -> none  [the longest x10 36.1 us: extended(): lax.ppermute(tail, axis, [(i, (i + 1) % count) for i in range(ends)])]
    all_to_all x8 -> x0, starting transfers between devices: 41.8 us -> none  [the longest x3 14.8 us: adjoint(): lax.all_to_all(spread.reshape(devices, capacity, ray_len), ('lat', 'rad')...]
    dot_general x6 -> x0, matrix products: 30.6 us -> none  [the longest x3 16.9 us: body(): jnp.einsum('sqrc,sqc->sqr', held_tiles, blocks, preferred_element_type=jn...]
    scatter x5 -> x0, local copies, waits for them, and re-layouts: 23 us -> none  [the longest x1 19.3 us: body(): outgoing.at[position].set(kernel.reshape(entries, ray_len, cell_len))]
    ppermute x20 -> x0, waiting for transfers between devices: 8.79 us -> none  [the longest x10 8.76 us: extended(): lax.ppermute(head, axis, [((i + 1) % count, i) for i in range(ends)])]
  transfers between devices with their start and end apart: 28 -> 0, of which waited for: 9 -> 0; matrix products, arithmetic and copies ran while one was open for 10% -> 0% of each run, Pallas kernels for 0% -> 0%
where the time goes in v1:
time: 65.5 us; the launch traced here: 65.1 us
  Pallas kernels  57.4 us (88%)
  local copies, waits for them, and re-layouts  7.06 us (11%)
    pallas_call x1, Pallas kernels, body(): pl.pallas_call(functools.partial(lsqr_kernel, n_lat, n_rad, slots), out_s...  57.4 us
    unnamed x12, local copies, waits for them, and re-layouts  7.06 us

profile of v1, /device:TPU:0, one launch (start us, length us, event | category | flops | bytes accessed | tf_op | source)
XLA Modules:
  0.0 65.1 jit_solution(7589687226729492739)
XLA Ops:
  0.6 0.8 %copy.8.target_ref = s32[32,4]{1,0:T(8,128)S(1)} copy(s32[32,4]{0,1:T(4,128)} %param.7) | data formatting | bytes 1024 | tf_op args[1]
  1.4 0.8 %copy.9.block_ref = s32[32,4]{1,0:T(8,128)S(1)} copy(s32[32,4]{0,1:T(4,128)} %param.8) | data formatting | bytes 1024 | tf_op args[2]
  2.2 0.0 copy-start
  2.2 2.2 %copy-done = bf16[32,4,64,256]{3,2,1,0:T(8,128)(2,1)S(1)} copy-done((bf16[32,4,64,256]{3,2,1,0:T(8,128)(2,1)S(1)}, bf16[32,4,64,256]{3,2,1,0:T(8,128)(2,1)}, u32[]{:S(2)}) %copy-start) | copy-done | bytes 4194328
  4.3 0.0 copy-start.1
  4.3 0.7 %copy-done.1 = f32[32,64]{1,0:T(8,128)S(1)} copy-done((f32[32,64]{1,0:T(8,128)S(1)}, f32[32,64]{1,0:T(8,128)}, u32[]{:S(2)}) %copy-start.1) | copy-done | bytes 8216
  5.1 0.0 copy-start.2
  5.1 0.7 %copy-done.2 = f32[32,64]{1,0:T(8,128)S(1)} copy-done((f32[32,64]{1,0:T(8,128)S(1)}, f32[32,64]{1,0:T(8,128)}, u32[]{:S(2)}) %copy-start.2) | copy-done | bytes 8216
  5.8 0.0 copy-start.3
  5.8 0.7 %copy-done.3 = s32[32]{0:T(128)S(1)} copy-done((s32[32]{0:T(128)S(1)}, s32[32]{0:T(128)}, u32[]{:S(2)}) %copy-start.3) | copy-done | bytes 152
  6.4 57.4 %shard_map.77 = (f32[8,16,256]{2,1,0:T(8,128)S(1)}, f32[32,64]{1,0:T(8,128)S(1)}) custom-call(bf16[32,4,64,256]{3,2,1,0:T(8,128)(2,1)S(1)} %copy-done, s32[32,4]{1,0:T(8,128)S(1)} %copy.8.target_ref, s32[32,4]{1,0:T(8,128)S(1)} %copy.9.block_ref, s32[1,32]{1,0:T(1,128)S(1)} %bitcast.1, f32[32,64]{1,0:T(8,128)S(1)} %copy-done.1, f32[32,64]{1,0:T(8,128)S(1)} %copy-done.2), custom_call_target="tpu_custom_call" | custom-call | flops 29360128 | bytes 4194304 | tf_op jit(solution)/shard_map/pallas_call | solution.py:355
  63.8 0.7 %copy.12 = f32[8,16,256]{2,1,0:T(8,128)} copy(f32[8,16,256]{2,1,0:T(8,128)S(1)} %get-tuple-element.4) | data formatting | bytes 262144
  64.5 0.6 copy.13
Async XLA Ops:
  2.2 2.2 %copy-start = (bf16[32,4,64,256]{3,2,1,0:T(8,128)(2,1)S(1)}, bf16[32,4,64,256]{3,2,1,0:T(8,128)(2,1)}, u32[]{:S(2)}) copy-start(bf16[32,4,64,256]{3,2,1,0:T(8,128)(2,1)} %kernel_ref.1) | copy-start | bytes 12582916
  4.3 0.7 %copy-start.1 = (f32[32,64]{1,0:T(8,128)S(1)}, f32[32,64]{1,0:T(8,128)}, u32[]{:S(2)}) copy-start(f32[32,64]{1,0:T(8,128)} %times_ref.1) | copy-start | bytes 24580
  5.1 0.7 %copy-start.2 = (f32[32,64]{1,0:T(8,128)S(1)}, f32[32,64]{1,0:T(8,128)}, u32[]{:S(2)}) copy-start(f32[32,64]{1,0:T(8,128)} %prior_ref.1) | copy-start | bytes 24580
  5.8 0.7 %copy-start.3 = (s32[32]{0:T(128)S(1)}, s32[32]{0:T(128)}, u32[]{:S(2)}) copy-start(s32[32]{0:T(128)} %param.9) | copy-start | bytes 388

commit v2 on v1

--- a/solution.py
+++ b/solution.py
@@ -30,11 +30,13 @@
 
 def lsqr_kernel(
     n_lat, n_rad, slots,
-    kernel_ref, target_ref, block_ref, counts_ref, times_ref, prior_ref,
+    kernel_ref, target_hbm, block_hbm, counts_hbm, times_hbm, prior_hbm,
     update_ref, data_ref,
-    tiles, send, recv, sum_send, sum_recv, edge_send, edge_recv, ids_send, ids_recv,
-    tile_sem, send_sem, recv_sem, sum_send_sem, sum_recv_sem, edge_send_sem, edge_recv_sem,
-    ids_send_sem, ids_recv_sem,
+    tiles, target_ref, block_ref, counts_ref, times_ref, prior_ref,
+    send, recv, rad_send, rad_recv, lat_send, lat_recv,
+    edge_send, edge_recv, ids_send, ids_recv,
+    tile_sem, small_sem, send_sem, recv_sem, rad_send_sem, rad_recv_sem,
+    lat_send_sem, lat_recv_sem, edge_send_sem, edge_recv_sem, ids_send_sem, ids_recv_sem,
 ):
     n = n_lat * n_rad
     rays_b, fanout, ray_len, cells = tiles.shape
@@ -45,21 +47,13 @@
     groups = rays_b // GROUP
     width = GROUP * ray_len
     lat, rad = lax.axis_index("lat"), lax.axis_index("rad")
-    me = lat * n_rad + rad
-
-    def at(peer):
-        return (peer // n_rad, peer % n_rad)
-
-    def shifted(step):
-        return at(lax.rem(me + step, n))
-
-    barrier = pltpu.get_barrier_semaphore()
-
-    def greet(step, carry):
-        pl.semaphore_signal(barrier, inc=1, device_id=shifted(step), device_id_type=MESH)
-        return carry
-
-    lax.fori_loop(1, n, greet, 0)
+
+    small = (
+        (target_hbm, target_ref), (block_hbm, block_ref), (counts_hbm, counts_ref),
+        (times_hbm, times_ref), (prior_hbm, prior_ref),
+    )
+    for i, (src, dst) in enumerate(small):
+        pltpu.make_async_copy(src, dst, small_sem.at[i]).start()
 
     def tile_copy(g):
         part = pl.ds(g * GROUP, GROUP)
@@ -68,28 +62,55 @@
     for g in range(groups):
         tile_copy(g).start()
 
-    named = jnp.concatenate([target_ref[:, k:k + 1] for k in range(fanout)], axis=0)
-    wanted = jnp.concatenate([block_ref[:, k:k + 1] for k in range(fanout)], axis=0)
-    away = named - me
-    away = jnp.where(away < 0, away + n, away)
+    rads = [lax.rem(rad + dr, n_rad) for dr in range(n_rad)]
+
+    def each_lat(act):
+        def go(dl, carry):
+            act(dl, lax.rem(lat + dl, n_lat))
+            return carry
+        lax.fori_loop(1, n_lat, go, 0)
+
+    def each_partner(act):
+        for dr in range(1, n_rad):
+            act(dr, n_rad - dr, (lat, rads[dr]))
+
+        def row(dl, peer):
+            here, there = dl * n_rad, (n_lat - dl) * n_rad
+            for dr in range(n_rad):
+                act(here + dr, there + (n_rad - dr) % n_rad, (peer, rads[dr]))
+        each_lat(row)
+
+    barrier = pltpu.get_barrier_semaphore()
+    each_partner(
+        lambda here, there, device: pl.semaphore_signal(
+            barrier, inc=1, device_id=device, device_id_type=MESH
+        )
+    )
+    for i, (src, dst) in enumerate(small):
+        pltpu.make_async_copy(src, dst, small_sem.at[i]).wait()
+
     square = (entries, entries)
-    away_col = jnp.broadcast_to(away.astype(F32), square)
-    away_row = away_col.T
+    named = jnp.concatenate([target_ref[k:k + 1, :] for k in range(fanout)], axis=1)
+    wanted = jnp.concatenate([block_ref[k:k + 1, :] for k in range(fanout)], axis=1)
+    away_lat = named // n_rad - lat
+    away_rad = named % n_rad - rad
+    away_lat = jnp.where(away_lat < 0, away_lat + n_lat, away_lat)
+    away_rad = jnp.where(away_rad < 0, away_rad + n_rad, away_rad)
+    away_row = jnp.broadcast_to((away_lat * n_rad + away_rad).astype(F32), square)
+    away_col = away_row.T
+    wanted = jnp.broadcast_to(wanted.astype(F32), square).T[:, 0:1]
     earlier = (away_col == away_row) & (iota(square, 1) < iota(square, 0))
     rank = jnp.sum(jnp.where(earlier, 1.0, 0.0), axis=1, keepdims=True)
-    place_col = away.astype(F32) * rows + rank
+    place_col = away_col[:, 0:1] * rows + rank
     place_row = jnp.broadcast_to(place_col, square).T[0:1, :]
     place_cols = jnp.concatenate([place_col + h * slots for h in range(halves)], axis=0)
     place_rows = jnp.concatenate([place_row + h * slots for h in range(halves)], axis=1)
-    pick = onehot(
-        iota((halves * entries, n * rows), 1) == place_cols.astype(jnp.int32)
-    )
     spread = onehot(
         iota((n * rows, halves * entries), 0) == place_rows.astype(jnp.int32)
     )
     partner = onehot(iota((n, entries), 0) == away_row[0:1, :].astype(jnp.int32))
     marks = jnp.where(
-        iota((entries, LANES), 1) == rank.astype(jnp.int32), (wanted + 1).astype(F32), 0.0
+        iota((entries, LANES), 1) == rank.astype(jnp.int32), wanted + 1.0, 0.0
     ).astype(BF16)
     ids = jnp.dot(partner, marks, preferred_element_type=F32)
 
@@ -123,39 +144,49 @@
     pl.semaphore_wait(barrier, n - 1)
 
     def exchange(src, dst, size, s_sem, r_sem):
-        def go(step, carry):
-            back = n - step
+        def part(i):
+            i = i * size
+            return pl.ds(i if isinstance(i, int) else pl.multiple_of(i, size), size)
+
+        def act(here, there, device):
             pltpu.make_async_remote_copy(
-                src_ref=src.at[pl.ds(pl.multiple_of(step * size, size), size)],
-                dst_ref=dst.at[pl.ds(pl.multiple_of(back * size, size), size)],
-                send_sem=s_sem, recv_sem=r_sem,
-                device_id=shifted(step), device_id_type=MESH,
+                src_ref=src.at[part(here)], dst_ref=dst.at[part(there)],
+                send_sem=s_sem, recv_sem=r_sem, device_id=device, device_id_type=MESH,
             ).start()
-            return carry
-        lax.fori_loop(1, n, go, 0)
-
-    def arrived(dst, size, sem):
-        part = dst.at[pl.ds(size, (n - 1) * size)]
+        each_partner(act)
+
+    def arrived(dst, size, sem, count=n):
+        part = dst.at[pl.ds(size, (count - 1) * size)]
         pltpu.make_async_copy(part, part, sem).wait()
 
     def send_sum(i, value):
         row = jnp.broadcast_to(value, (1, LANES))
-        sum_send[i] = row
-        sum_recv[i, 0] = row
-        src, dst = sum_send.at[i], sum_recv.at[i]
-
-        def go(step, carry):
+        rad_send[i] = row
+        rad_recv[i, 0] = row
+        for dr in range(1, n_rad):
             pltpu.make_async_remote_copy(
-                src_ref=src, dst_ref=dst.at[n - step],
-                send_sem=sum_send_sem.at[i], recv_sem=sum_recv_sem.at[i],
-                device_id=shifted(step), device_id_type=MESH,
+                src_ref=rad_send.at[i], dst_ref=rad_recv.at[i, n_rad - dr],
+                send_sem=rad_send_sem.at[i], recv_sem=rad_recv_sem.at[i],
+                device_id=(lat, rads[dr]), device_id_type=MESH,
             ).start()
-            return carry
-        lax.fori_loop(1, n, go, 0)
+
+    def pass_sum(i):
+        arrived(rad_recv.at[i], 1, rad_recv_sem.at[i], n_rad)
+        row = jnp.sum(rad_recv[i], axis=0)
+        lat_send[i] = row
+        lat_recv[i, 0] = row
+
+        def act(dl, peer):
+            pltpu.make_async_remote_copy(
+                src_ref=lat_send.at[i], dst_ref=lat_recv.at[i, n_lat - dl],
+                send_sem=lat_send_sem.at[i], recv_sem=lat_recv_sem.at[i],
+                device_id=(peer, rad), device_id_type=MESH,
+            ).start()
+        each_lat(act)
 
     def get_sum(i):
-        arrived(sum_recv.at[i], 1, sum_recv_sem.at[i])
-        return jnp.sum(sum_recv[i], axis=0)[:, 0:1]
+        arrived(lat_recv.at[i], 1, lat_recv_sem.at[i], n_lat)
+        return jnp.sum(lat_recv[i], axis=0)[:, 0:1]
 
     field4 = (halves, MB_R, MB_L, LANES)
     field = (halves * num_blocks, LANES)
@@ -213,10 +244,10 @@
         recv[i, 0:rows] = send[i, 0:rows]
         exchange(send.at[i], recv.at[i], rows, send_sem.at[i], recv_sem.at[i])
 
-    def adjoint(i, ray_values, first=False):
+    def adjoint(i, ray_values, sum_i=None):
         parts = [[None] * groups for _ in range(fanout)]
         for g in range(groups):
-            if first:
+            if sum_i is None:
                 tile_copy(g).wait()
             y = ray_values[g].astype(BF16)
             for k in range(fanout):
@@ -225,6 +256,8 @@
         stacked = jnp.concatenate(
             [p[:, h * LANES:(h + 1) * LANES] for h in range(halves) for p in flat], axis=0
         ).astype(BF16)
+        if sum_i is not None:
+            pass_sum(sum_i)
         send_rows(i, jnp.dot(spread, stacked, preferred_element_type=F32))
 
     def forward(i):
@@ -255,7 +288,11 @@
     ids_recv[0] = ids_send[0]
     exchange(ids_send, ids_recv, 1, ids_send_sem, ids_recv_sem)
 
-    adjoint(0, [w * d for w, d in zip(weights, data)], first=True)
+    adjoint(0, [w * d for w, d in zip(weights, data)])
+
+    pick = onehot(
+        iota((halves * entries, n * rows), 1) == place_cols.astype(jnp.int32)
+    )
 
     arrived(ids_recv, 1, ids_recv_sem)
     got = ids_recv[...].reshape(n, LANES)
@@ -280,15 +317,17 @@
     round_i, sum_i, edge_i = 1, 0, 0
     pen = search = update = None
     for sweep in range(ITERS):
-        send_rows(round_i, jnp.dot(gather, x.astype(BF16), preferred_element_type=F32))
         send_edges(edge_i, x)
         send_sum(sum_i, total([x]))
+        send_rows(round_i, jnp.dot(gather, x.astype(BF16), preferred_element_type=F32))
+        pass_sum(sum_i)
+        rough = DAMPING * roughen(edge_i, x)
         products = forward(round_i)
         alpha = jnp.sqrt(get_sum(sum_i))
         inverse = 1.0 / alpha
         data = [w * (p * inverse) - alpha * d for w, p, d in zip(weights, products, data)]
         v = x * inverse
-        pen_new = (DAMPING * inverse) * roughen(edge_i, x)
+        pen_new = inverse * rough
         pen = pen_new if pen is None else pen_new - alpha * pen
         round_i, sum_i, edge_i = round_i + 1, sum_i + 1, edge_i + 1
         if sweep == 0:
@@ -302,7 +341,9 @@
         send_sum(sum_i, acc)
         if not last:
             send_edges(edge_i, pen)
-            adjoint(round_i, [w * d for w, d in zip(weights, data)])
+            adjoint(round_i, [w * d for w, d in zip(weights, data)], sum_i)
+        else:
+            pass_sum(sum_i)
         beta = jnp.sqrt(get_sum(sum_i))
         inverse = 1.0 / beta
         data = [d * inverse for d in data]
@@ -313,9 +354,9 @@
         step = (phi / rho) * search
         update = step if update is None else update + step
         if not last:
-            rough = DAMPING * roughen(edge_i, pen)
+            rest = (DAMPING * inverse) * roughen(edge_i, pen) - beta * v
             pen = pen * inverse
-            x = (collected(round_i) + rough) * inverse - beta * v
+            x = collected(round_i) * inverse + rest
             round_i, edge_i = round_i + 1, edge_i + 1
         sum_i += 1
 
@@ -335,7 +376,8 @@
     for i in range(2 * ITERS):
         left_buffer(send.at[i, pl.ds(rows, (n - 1) * rows)], send_sem.at[i])
     for i in range(2 * ITERS):
-        left_buffer(sum_recv.at[i, pl.ds(1, n - 1)], sum_send_sem.at[i])
+        left_buffer(rad_recv.at[i, pl.ds(1, n_rad - 1)], rad_send_sem.at[i])
+        left_buffer(lat_recv.at[i, pl.ds(1, n_lat - 1)], lat_send_sem.at[i])
     for i in range(2 * ITERS - 1):
         left_buffer(edge_send.at[i], edge_send_sem.at[i])
 
@@ -352,37 +394,44 @@
     payloads, sums, fields = 2 * ITERS, 2 * ITERS, 2 * ITERS - 1
     dma = pltpu.SemaphoreType.DMA
     vmem = pl.BlockSpec(memory_space=pltpu.VMEM)
+    operands = (
+        kernel, target_device.T, target_block.T, counts.reshape(1, rays_b),
+        traveltimes, prior_residual,
+    )
     return pl.pallas_call(
         functools.partial(lsqr_kernel, n_lat, n_rad, slots),
         out_shape=(
             jax.ShapeDtypeStruct((MB_R, MB_L, cells), F32),
             jax.ShapeDtypeStruct((rays_b, ray_len), F32),
         ),
-        in_specs=[pl.BlockSpec(memory_space=pl.ANY)] + [vmem] * 5,
+        in_specs=[pl.BlockSpec(memory_space=pltpu.HBM)] * len(operands),
         out_specs=(vmem, vmem),
         scratch_shapes=[
-            pltpu.VMEM(kernel.shape, BF16),
+            *[pltpu.VMEM(a.shape, a.dtype) for a in operands],
             pltpu.VMEM((payloads, n * rows, LANES), BF16),
             pltpu.VMEM((payloads, n * rows, LANES), BF16),
             pltpu.VMEM((sums, 1, LANES), F32),
-            pltpu.VMEM((sums, n, 1, LANES), F32),
+            pltpu.VMEM((sums, n_rad, 1, LANES), F32),
+            pltpu.VMEM((sums, 1, LANES), F32),
+            pltpu.VMEM((sums, n_lat, 1, LANES), F32),
             pltpu.VMEM((fields, edges, LANES), F32),
             pltpu.VMEM((fields, edges, LANES), F32),
             pltpu.VMEM((n, 1, LANES), F32),
             pltpu.VMEM((n, 1, LANES), F32),
             dma((rays_b // GROUP,)),
+            dma((len(operands) - 1,)),
             dma((payloads,)), dma((payloads,)),
-            dma((sums,)), dma((sums,)),
+            dma((sums,)), dma((sums,)), dma((sums,)), dma((sums,)),
             dma((fields,)), dma((fields,)),
             dma, dma,
         ],
         compiler_params=pltpu.CompilerParams(
-            collective_id=0, has_side_effects=True, vmem_limit_bytes=48 * 1024 * 1024
+            collective_id=0, has_side_effects=True, vmem_limit_bytes=64 * 1024 * 1024
         ),
         cost_estimate=pl.CostEstimate(
             flops=14 * kernel.size, bytes_accessed=2 * kernel.size, transcendentals=0
         ),
-    )(kernel, target_device, target_block, counts.reshape(1, rays_b), traveltimes, prior_residual)
+    )(*operands)
 
 
 def solution(mesh):

time: 65.5 us -> 65.2 us (level)
  local copies, waits for them, and re-layouts: 7.06 us -> 2.89 us
  Pallas kernels: 57.4 us -> 61.4 us
    unnamed x12 -> x2, local copies, waits for them, and re-layouts: 7.06 us -> 2.89 us
    pallas_call x1, Pallas kernels: 57.4 us -> 61.4 us  [body(): pl.pallas_call(functools.partial(lsqr_kernel, n_lat, n_rad, slots), out_s...]
where the time goes in v2:
time: 65.2 us; the launch traced here: 64.9 us
  Pallas kernels  61.4 us (94%)
  local copies, waits for them, and re-layouts  2.89 us (4%)
    pallas_call x1, Pallas kernels, body(): pl.pallas_call(functools.partial(lsqr_kernel, n_lat, n_rad, slots), out_s...  61.4 us
    unnamed x2, local copies, waits for them, and re-layouts  2.89 us

profile of v2, /device:TPU:0, one launch (start us, length us, event | category | flops | bytes accessed | tf_op | source)
XLA Modules:
  0.0 64.9 jit_solution(1361226221426548116)
XLA Ops:
  0.6 61.4 %shard_map.77 = (f32[8,16,256]{2,1,0:T(8,128)}, f32[32,64]{1,0:T(8,128)}) custom-call(bf16[32,4,64,256]{3,2,1,0:T(8,128)(2,1)} %kernel_ref.1, s32[4,32]{1,0:T(4,128)} %bitcast.3, s32[4,32]{1,0:T(4,128)} %bitcast.4, s32[1,32]{1,0:T(1,128)} %bitcast.5, f32[32,64]{1,0:T(8,128)} %times_hbm.1, f32[32,64]{1,0:T(8,128)} %prior_hbm.1), custom_call_target="tpu_custom_call" | custom-call | flops 29360128 | bytes 4194304 | tf_op jit(solution)/shard_map/pallas_call | solution.py:401
  62.0 1.6 %copy.10 = f32[8,16,256]{2,1,0:T(8,128)} copy(f32[8,16,256]{2,1,0:T(8,128)} %get-tuple-element.4) | data formatting | bytes 262144
  63.6 1.3 %copy.11 = f32[32,64]{1,0:T(8,128)} copy(f32[32,64]{1,0:T(8,128)} %get-tuple-element.5) | data formatting | bytes 16384

commit v3 on v2

--- a/solution.py
+++ b/solution.py
@@ -317,9 +317,9 @@
     round_i, sum_i, edge_i = 1, 0, 0
     pen = search = update = None
     for sweep in range(ITERS):
+        send_rows(round_i, jnp.dot(gather, x.astype(BF16), preferred_element_type=F32))
+        send_sum(sum_i, total([x]))
         send_edges(edge_i, x)
-        send_sum(sum_i, total([x]))
-        send_rows(round_i, jnp.dot(gather, x.astype(BF16), preferred_element_type=F32))
         pass_sum(sum_i)
         rough = DAMPING * roughen(edge_i, x)
         products = forward(round_i)
@@ -426,12 +426,12 @@
             dma, dma,
         ],
         compiler_params=pltpu.CompilerParams(
-            collective_id=0, has_side_effects=True, vmem_limit_bytes=64 * 1024 * 1024
+            collective_id=0, has_side_effects=True, vmem_limit_bytes=48 * 1024 * 1024
         ),
         cost_estimate=pl.CostEstimate(
             flops=14 * kernel.size, bytes_accessed=2 * kernel.size, transcendentals=0
         ),
-    )(*operands)
+    )(*[pltpu.with_memory_space_constraint(a, pltpu.HBM) for a in operands])
 
 
 def solution(mesh):

time: 65.2 us -> 63.9 us (0.980)
  local copies, waits for them, and re-layouts: 2.89 us -> 1.26 us
    unnamed x2, local copies, waits for them, and re-layouts: 2.89 us -> 1.26 us
where the time goes in v3:
time: 63.9 us; the launch traced here: 63.7 us
  Pallas kernels  61.8 us (97%)
  local copies, waits for them, and re-layouts  1.26 us (2%)
  between operations  0.64 us (1%)
    pallas_call x1, Pallas kernels, body(): pl.pallas_call(functools.partial(lsqr_kernel, n_lat, n_rad, slots), out_s...  61.8 us

profile of v3, /device:TPU:0, one launch (start us, length us, event | category | flops | bytes accessed | tf_op | source)
XLA Modules:
  0.0 63.7 jit_solution(5105988732390486406)
XLA Ops:
  0.6 61.8 %shard_map.77 = (f32[8,16,256]{2,1,0:T(8,128)S(1)}, f32[32,64]{1,0:T(8,128)S(1)}) custom-call(bf16[32,4,64,256]{3,2,1,0:T(8,128)(2,1)} %kernel_ref.1, s32[4,32]{1,0:T(4,128)} %bitcast.3, s32[4,32]{1,0:T(4,128)} %bitcast.4, s32[1,32]{1,0:T(1,128)} %bitcast.5, f32[32,64]{1,0:T(8,128)} %times_hbm.1, f32[32,64]{1,0:T(8,128)} %prior_hbm.1), custom_call_target="tpu_custom_call" | custom-call | flops 29360128 | bytes 4194304 | tf_op jit(solution)/shard_map/pallas_call | solution.py:401
  62.4 0.7 %copy.10 = f32[8,16,256]{2,1,0:T(8,128)} copy(f32[8,16,256]{2,1,0:T(8,128)S(1)} %get-tuple-element.4) | data formatting | bytes 262144
  63.1 0.6 copy.11

commit v4 on v3

--- a/solution.py
+++ b/solution.py
@@ -65,20 +65,20 @@
     rads = [lax.rem(rad + dr, n_rad) for dr in range(n_rad)]
 
     def each_lat(act):
-        def go(dl, carry):
+        def go(i, carry):
+            dl = n_lat // 2 + (2 * lax.rem(i, 2) - 1) * ((i + 1) // 2)
             act(dl, lax.rem(lat + dl, n_lat))
             return carry
-        lax.fori_loop(1, n_lat, go, 0)
+        lax.fori_loop(0, n_lat - 1, go, 0)
 
     def each_partner(act):
-        for dr in range(1, n_rad):
-            act(dr, n_rad - dr, (lat, rads[dr]))
-
         def row(dl, peer):
             here, there = dl * n_rad, (n_lat - dl) * n_rad
             for dr in range(n_rad):
                 act(here + dr, there + (n_rad - dr) % n_rad, (peer, rads[dr]))
         each_lat(row)
+        for dr in range(1, n_rad):
+            act(dr, n_rad - dr, (lat, rads[dr]))
 
     barrier = pltpu.get_barrier_semaphore()
     each_partner(

time: 63.9 us -> 64.2 us (level)
  no operation moved by 1% of the time
where the time goes in v4:
time: 64.2 us; the launch traced here: 64 us
  Pallas kernels  62.1 us (97%)
  local copies, waits for them, and re-layouts  1.26 us (2%)
    pallas_call x1, Pallas kernels, body(): pl.pallas_call(functools.partial(lsqr_kernel, n_lat, n_rad, slots), out_s...  62.1 us

profile of v4, /device:TPU:0, one launch (start us, length us, event | category | flops | bytes accessed | tf_op | source)
XLA Modules:
  0.0 64.0 jit_solution(18010684129046286224)
XLA Ops:
  0.6 62.1 %shard_map.77 = (f32[8,16,256]{2,1,0:T(8,128)S(1)}, f32[32,64]{1,0:T(8,128)S(1)}) custom-call(bf16[32,4,64,256]{3,2,1,0:T(8,128)(2,1)} %kernel_ref.1, s32[4,32]{1,0:T(4,128)} %bitcast.3, s32[4,32]{1,0:T(4,128)} %bitcast.4, s32[1,32]{1,0:T(1,128)} %bitcast.5, f32[32,64]{1,0:T(8,128)} %times_hbm.1, f32[32,64]{1,0:T(8,128)} %prior_hbm.1), custom_call_target="tpu_custom_call" | custom-call | flops 29360128 | bytes 4194304 | tf_op jit(solution)/shard_map/pallas_call | solution.py:401
  62.7 0.7 %copy.10 = f32[8,16,256]{2,1,0:T(8,128)} copy(f32[8,16,256]{2,1,0:T(8,128)S(1)} %get-tuple-element.4) | data formatting | bytes 262144
  63.4 0.6 copy.11
